TPU v7x, 32 devices: a whole 2x2x4 slice. The times are simulated.
32 devices in a mesh: groups: 2 (over x), pair: 16 (over z, y, core).
Axes of the slice: x: 2, y: 2, z: 4, core: 2. Of those that a mesh axis runs over, the one named last changes fastest.
Arguments:
- t2_amp: float32 [128, 8, 9216], P(('groups', 'pair')), parts along dimension 0, may hold values from -6 to 6
- ladder_ints: bfloat16 [147456, 9216], P(('groups', 'pair')), parts along dimension 0, may hold values from -0.0625 to 0.0625
- fock_vv: float32 [16, 96, 96], P('groups'), parts along dimension 0, may hold values from -0.625 to 0.625
- vir_energy: float32 [16, 96], P('groups'), parts along dimension 0, may hold values from 0.5 to 4
- occ_energy: float32 [300], P('groups'), parts along dimension 0, may hold values from -3 to -0.5
- vir_sizes: int32 [16], P('groups'), parts along dimension 0, may hold values from 48 to 96, as said below
- pair_index: int32 [128, 2], P(('groups', 'pair')), parts along dimension 0, may hold values from 0 to 149, as said below
Outputs:
- increment: float32 [128, 8, 9216], P(('groups', 'pair')), parts along dimension 0
There are 2 independent parts, one for each index of `groups`. A program takes and returns all parts, laid end to end along the dimension named above; each array names one. Nothing has to cross between parts.
Inputs may be any that keep to these rules, and one draw needn't show every extreme that they name: `vir_sizes`: at least one irrep block is full. `pair_index`: each pair has i <= j.
All inputs are finite; a program needn't handle non-finite values.
Results may differ from a plain program's by a relative error of at most 0.0016.
Values may be sent and summed in bfloat16 or wider, within the bound.
No kernel may reach another device: no remote copies, remote signals or barrier semaphores. Data moves between devices by JAX's collectives and lax.ppermute only.
A program may use at most 192 MiB of HBM per device.

v0:
```python
import functools

import jax
import jax.numpy as jnp
from jax import lax
from jax.experimental import pallas as pl
from jax.experimental.pallas import tpu as pltpu
from jax.sharding import PartitionSpec as P

CONTRACT_LAST = (((1,), (1,)), ((), ()))
VMEM_BYTES = 48 * 1024 * 1024
IN_VMEM = pl.BlockSpec(memory_space=pltpu.VMEM)
IN_SMEM = pl.BlockSpec(memory_space=pltpu.SMEM)
ANYWHERE = pl.BlockSpec(memory_space=pl.ANY)


def tile_of(rows, most):
    for size in range(most - most % 128, 0, -128):
        if rows % size == 0:
            return size
    return rows


def block_kernel(sizes_ref, amps_ref, copies_ref, sizes, amps, arrived, *, width):
    arrivals = [
        pltpu.make_async_copy(sizes_ref, sizes, arrived.at[0]),
        pltpu.make_async_copy(amps_ref, amps, arrived.at[1]),
    ]
    for arrival in arrivals:
        arrival.start()
    spot = lax.broadcasted_iota(jnp.int32, (1, amps_ref.shape[2]), 1)
    c = ((spot.astype(jnp.float32) + 0.5) * (1.0 / width)).astype(jnp.int32)
    d = spot - c * width
    for arrival in arrivals:
        arrival.wait()
    live = (c < sizes[0]) & (d < sizes[0])
    block = jnp.where(live, amps[:, 0, :], 0.0).astype(jnp.bfloat16)
    for copy in range(copies_ref.shape[0]):
        copies_ref[copy] = block


def block_copies(sizes, amps, chips, width):
    pairs, _, columns = amps.shape
    return pl.pallas_call(
        functools.partial(block_kernel, width=width),
        in_specs=[ANYWHERE, ANYWHERE],
        out_specs=IN_VMEM,
        out_shape=jax.ShapeDtypeStruct((chips, pairs, columns), jnp.bfloat16),
        scratch_shapes=[
            pltpu.SMEM(sizes.shape, sizes.dtype),
            pltpu.VMEM(amps.shape, amps.dtype),
            pltpu.SemaphoreType.DMA((2,)),
        ],
        compiler_params=pltpu.CompilerParams(vmem_limit_bytes=63 * 1024 * 1024),
        name="block_copies",
    )(sizes, amps)


def ladder_kernel(sizes_ref, own_ref, other_ref, ints_ref, out_ref, amps, slots, total, arrived, *, orbitals, stripe):
    depth, tile, columns = slots.shape
    tiles = out_ref.shape[2] // tile
    each = out_ref.shape[1]
    live = sizes_ref[0] * orbitals
    least = columns // (2 * stripe)
    most = columns // stripe
    steps = jnp.int32(least)
    for step in range(least, most):
        steps += (live > step * stripe).astype(jnp.int32)

    def fetch(width, slot, place):
        return pltpu.make_async_copy(
            ints_ref.at[pl.ds(pl.multiple_of(place * tile, tile), tile), pl.ds(0, width)],
            slots.at[slot, :, pl.ds(0, width)],
            arrived.at[slot],
        )

    def begin(width):
        for slot in range(min(depth - 1, tiles)):
            fetch(width, slot, slot).start()

    def store(place):
        ladder = total[...].T
        spot = pl.ds(pl.multiple_of(place * tile, 128), tile)
        for device in range(out_ref.shape[0]):
            out_ref[device, :, spot] = ladder[device * each : (device + 1) * each].astype(
                out_ref.dtype
            )

    def run(width):
        def item(place, carry):
            slot = lax.rem(place, depth)
            fetch(width, slot, place).wait()

            @pl.when(place + depth - 1 < tiles)
            def _():
                fetch(width, lax.rem(place + depth - 1, depth), place + depth - 1).start()

            store(jnp.maximum(place - 1, 0))
            total[...] = lax.dot_general(
                slots[slot, :, :width],
                amps[:, :width],
                CONTRACT_LAST,
                preferred_element_type=jnp.float32,
            )
            return carry

        lax.fori_loop(0, tiles, item, 0)

    for count in range(least, most + 1):
        pl.when(steps == count)(functools.partial(begin, count * stripe))
    core = lax.rem(lax.axis_index("pair"), 2)
    own = own_ref[...].astype(jnp.float32)
    other = other_ref[...].astype(jnp.float32)
    both = [jnp.where(core == 0, own, other), jnp.where(core == 0, other, own)]
    amps[...] = jnp.concatenate(both, axis=1).reshape(amps.shape).astype(amps.dtype)
    total[...] = jnp.zeros_like(total)
    for count in range(least, most + 1):
        pl.when(steps == count)(functools.partial(run, count * stripe))
    store(tiles - 1)


def ladder_rows(sizes, own, other, ints, orbitals):
    chips, each, columns = own.shape
    pairs = 2 * chips * each
    rows = ints.shape[0]
    tile = tile_of(rows, 256)
    depth = 4 if tile <= 256 else 3
    return pl.pallas_call(
        functools.partial(ladder_kernel, orbitals=orbitals, stripe=columns // 12),
        in_specs=[IN_SMEM, IN_VMEM, IN_VMEM, ANYWHERE],
        out_specs=IN_VMEM,
        out_shape=jax.ShapeDtypeStruct((2 * chips, each, rows), jnp.bfloat16),
        scratch_shapes=[
            pltpu.VMEM((pairs, columns), jnp.bfloat16),
            pltpu.VMEM((depth, tile, columns), jnp.bfloat16),
            pltpu.VMEM((tile, pairs), jnp.float32),
            pltpu.SemaphoreType.DMA((depth,)),
        ],
        compiler_params=pltpu.CompilerParams(vmem_limit_bytes=VMEM_BYTES),
        cost_estimate=pl.CostEstimate(
            flops=2 * pairs * rows * columns, bytes_accessed=2 * rows * columns, transcendentals=0
        ),
        name="ladder_rows",
    )(sizes, own, other, ints)


def increment_kernel(ladder_ref, scale_ref, offset_ref, out_ref):
    devices, pairs, rows = ladder_ref.shape
    irreps = out_ref.shape[1]
    each = devices // irreps
    for pair in range(pairs):
        for piece in range(each):
            lines = [
                ladder_ref[irrep * each + piece, pair : pair + 1, :].astype(jnp.float32)
                for irrep in range(irreps)
            ]
            spot = slice(piece * rows, (piece + 1) * rows)
            out_ref[pair, :, spot] = (
                jnp.concatenate(lines, axis=0) * scale_ref[pair, :, spot] + offset_ref[pair, :, spot]
            )


def increments(ladder, scale, offset):
    if ladder.shape[2] % 128 or ladder.shape[0] % scale.shape[1]:
        ladder = jnp.swapaxes(ladder, 0, 1).reshape(scale.shape).astype(jnp.float32)
        return ladder * scale + offset
    return pl.pallas_call(
        increment_kernel,
        in_specs=[IN_VMEM] * 3,
        out_specs=IN_VMEM,
        out_shape=jax.ShapeDtypeStruct(scale.shape, scale.dtype),
        compiler_params=pltpu.CompilerParams(vmem_limit_bytes=VMEM_BYTES),
        name="increments",
    )(ladder, scale, offset)


def on_device(devices, t2_amp, ladder_ints, fock_vv, vir_energy, occ_energy, vir_sizes, pair_index):
    irreps = vir_energy.shape[0]
    width = vir_energy.shape[1]
    square = width * width
    pair_count = t2_amp.shape[0]
    same_core = [[2 * chip + core for chip in range(devices // 2)] for core in range(2)]
    other_core = [(device, device ^ 1) for device in range(devices)]
    copies = block_copies(vir_sizes, t2_amp, devices // 2, width)
    own = lax.all_to_all(
        copies, "pair", split_axis=0, concat_axis=0, axis_index_groups=same_core
    )
    live = jnp.arange(width, dtype=jnp.int32)[None, :] < vir_sizes[:, None]
    pair_live = (live[:, :, None] & live[:, None, :]).reshape(irreps, square)
    masked = jnp.where(pair_live[None], t2_amp, jnp.zeros_like(t2_amp))
    amps = masked.reshape(pair_count, irreps, width, width)
    fock = jnp.einsum("phac,hcb->phab", amps, fock_vv, precision=lax.Precision.HIGHEST)
    fock = fock + jnp.einsum("hac,phcb->phab", fock_vv, amps, precision=lax.Precision.HIGHEST)
    fock = fock.reshape(pair_count, irreps, square)
    own, fock = lax.optimization_barrier((own, fock))
    other = lax.ppermute(own, "pair", other_core)
    sent = ladder_rows(vir_sizes, own, other, ladder_ints, width)

    sent, fock, vir_energy, occ_energy = lax.optimization_barrier(
        (sent, fock, vir_energy, occ_energy)
    )
    ladder = lax.all_to_all(sent, "pair", split_axis=0, concat_axis=0)
    occupied = occ_energy.shape[0]
    matched = pair_index[:, :, None] == jnp.arange(occupied, dtype=jnp.int32)[None, None, :]
    chosen = jnp.sum(
        jnp.where(matched, occ_energy[None, None, :], jnp.zeros_like(occ_energy)[None, None, :]),
        axis=-1,
    )
    vir_pair = (vir_energy[:, :, None] + vir_energy[:, None, :]).reshape(irreps, square)
    denom = vir_pair[None] - (chosen[:, 0] + chosen[:, 1])[:, None, None]
    scale = jnp.where(pair_live[None], 1.0 / denom, 0.0)
    ladder, scale, offset = lax.optimization_barrier((ladder, scale, scale * fock))
    return increments(ladder, scale, offset)


def solution(mesh):
    in_specs = (
        P(("groups", "pair"), None, None),
        P(("groups", "pair"), None),
        P("groups", None, None),
        P("groups", None),
        P("groups"),
        P("groups"),
        P(("groups", "pair"), None),
    )
    out_specs = P(("groups", "pair"), None, None)
    return jax.shard_map(
        functools.partial(on_device, mesh.shape["pair"]),
        mesh=mesh,
        in_specs=in_specs,
        out_specs=out_specs,
        check_vma=False,
    )
```

profile of v0, /device:TPU:11, one launch (start us, length us, event | category | flops | bytes accessed | tf_op | source)
XLA Modules:
  0.0 76.8 jit_solution(18218196284764257099)
XLA Ops:
  0.0 2.3 %block_copies.1 = bf16[8,4,9216]{2,1,0:T(4,128)(2,1)} custom-call(s32[8]{0:T(128)} %sizes_ref.3, f32[4,8,9216]{2,1,0:T(8,128)} %amps_ref.1), custom_call_target="tpu_custom_call" | custom-call | tf_op jit(solution)/shard_map/block_copies/pallas_call | solution.py:44
  2.3 0.0 copy-start.2
  2.3 5.9 %all-to-all-start = ((bf16[8,4,9216]{2,1,0:T(4,128)(2,1)}), bf16[8,4,9216]{2,1,0:T(4,128)(2,1)S(1)}, u32[]{:S(2)}, u32[]{:S(2)}) async-start(bf16[8,4,9216]{2,1,0:T(4,128)(2,1)} %block_copies.1), calls=%async_computation | async-start | bytes 1179648 | tf_op jit(solution)/shard_map/all_to_all | solution.py:185
  8.2 0.1 iota_compare_fusion.1
  8.2 0.2 broadcast_and_fusion
  8.4 0.3 and.23
  8.7 1.1 %broadcast_select_fusion = f32[4,8,9216]{2,1,0:T(8,128)} fusion(f32[4,8,9216]{2,1,0:T(8,128)S(1)} %copy-done.2, pred[8,9216]{1,0:T(8,128)(4,1)S(1)} %and.23), kind=kLoop, calls=%fused_computation.5 | loop fusion | flops 294912 | bytes 2433024 | tf_op jit(solution)/shard_map/jit(_where)/select_n | solution.py:190
  9.8 1.9 %reshape.84 = f32[4,8,96,96]{3,2,1,0:T(8,128)S(1)} reshape(f32[4,8,9216]{2,1,0:T(8,128)} %broadcast_select_fusion) | data formatting | bytes 2359296 | tf_op jit(solution)/shard_map/reshape | solution.py:191
  11.7 1.5 %fusion.1 = f32[8,4,96,96]{3,2,1,0:T(8,128)S(1)} fusion(f32[4,8,96,96]{3,2,1,0:T(8,128)S(1)} %reshape.84, f32[8,96,96]{2,1,0:T(8,128)S(1)} %copy-done), kind=kOutput, calls=%fused_computation.2 | convolution fusion | flops 339738624 | bytes 2654208 | tf_op jit(solution)/shard_map/phac,hcb->phab/dot_general | solution.py:192
  13.2 2.7 %bitcast_add_fusion = f32[4,8,96,96]{3,2,0,1:T(8,128)} fusion(f32[8,4,96,96]{3,2,1,0:T(8,128)S(1)} %fusion.1, f32[4,8,96,96]{3,2,1,0:T(8,128)S(1)} %reshape.84, f32[8,96,96]{2,1,0:T(8,128)S(1)} %copy-done), kind=kOutput, calls=%fused_computation | convolution fusion | flops 340033536 | bytes 3833856 | tf_op jit(solution)/shard_map/hac,phcb->phab/dot_general | solution.py:193
  15.9 2.6 %reshape.87 = f32[4,8,9216]{2,0,1:T(4,128)S(1)} reshape(f32[4,8,96,96]{3,2,0,1:T(8,128)} %bitcast_add_fusion) | data formatting | bytes 2359296 | tf_op jit(solution)/shard_map/reshape | solution.py:194
  18.5 1.7 %copy.21 = f32[4,8,9216]{2,1,0:T(8,128)} copy(f32[4,8,9216]{2,0,1:T(4,128)S(1)} %reshape.87) | data formatting | bytes 2359296 | tf_op jit(solution)/shard_map/reshape | solution.py:194
  20.2 0.5 all-to-all-done.own_ref
  20.7 3.3 %collective-permute-start = (bf16[8,4,9216]{2,1,0:T(4,128)(2,1)S(1)}, bf16[8,4,9216]{2,1,0:T(4,128)(2,1)S(1)}, u32[]{:S(2)}, u32[]{:S(2)}) collective-permute-start(bf16[8,4,9216]{2,1,0:T(4,128)(2,1)S(1)} %all-to-all-done.own_ref), channel_id=1, source_target_pairs={{0,1},{1,0},{2,3},{3,2},{4,5},{5,4},{6,7},{7,6},{8,9},{9,8},{10,11... | collective-permute-start | bytes 1769480 | tf_op jit(solution)/shard_map/ppermute | solution.py:196
  23.9 1.6 %collective-permute-done.other_ref = bf16[8,4,9216]{2,1,0:T(4,128)(2,1)S(1)} collective-permute-done((bf16[8,4,9216]{2,1,0:T(4,128)(2,1)S(1)}, bf16[8,4,9216]{2,1,0:T(4,128)(2,1)S(1)}, u32[]{:S(2)}, u32[]{:S(2)}) %collective-permute-start) | collective-permute-done | bytes 589856 | tf_op jit(solution)/shard_map/ppermute | solution.py:196
  25.6 28.6 %ladder_rows.1 = bf16[16,4,4608]{2,1,0:T(4,128)(2,1)} custom-call(s32[8]{0:T(128)S(1)} %copy-done.1, bf16[8,4,9216]{2,1,0:T(4,128)(2,1)S(1)} %all-to-all-done.own_ref, bf16[8,4,9216]{2,1,0:T(4,128)(2,1)S(1)} %collective-permute-done.other_ref, bf16[4608,9216]{1,0:T(8,128)(2,1)} %ints_ref.1), custom_call_target="tpu_custom_call" | custom-call | flops 5435817984 | bytes 84934656 | tf_op jit(solution)/shard_map/ladder_rows/pallas_call | solution.py:128
  54.2 0.0 copy-start.3
  54.2 0.2 select_reduce_fusion
  54.4 5.0 %all-to-all-start.1 = ((bf16[16,4,4608]{2,1,0:T(4,128)(2,1)}), bf16[16,4,4608]{2,1,0:T(4,128)(2,1)S(1)}, u32[]{:S(2)}, u32[]{:S(2)}) async-start(bf16[16,4,4608]{2,1,0:T(4,128)(2,1)} %ladder_rows.1), calls=%async_computation.1 | async-start | bytes 1179648 | tf_op jit(solution)/shard_map/all_to_all | solution.py:202
  59.4 0.2 broadcast_add_fusion
  59.6 0.9 %add.37 = f32[8,9216]{1,0:T(8,128)} reshape(f32[8,96,96]{2,1,0:T(8,128)S(1)} %broadcast_add_fusion) | data formatting | bytes 589824 | tf_op jit(solution)/shard_map/add | solution.py:209
  60.5 1.6 %fusion.5 = (f32[4,8,9216]{2,1,0:T(8,128)S(1)}, f32[4,8,9216]{2,1,0:T(8,128)S(1)}) fusion(f32[4,8,9216]{2,1,0:T(8,128)} %copy.21, f32[4]{0:T(128)S(1)} %add_bitcast_fusion, f32[8,9216]{1,0:T(8,128)} %add.37, pred[8,9216]{1,0:T(8,128)(4,1)S(1)} %and.23), kind=kLoop, calls=%fused_computation.10 | loop fusion | flops 1179648 | bytes 3907600 | tf_op jit(solution)/shard_map/mul | solution.py:212
  62.1 12.9 %all-to-all-done.1.ladder_ref = bf16[16,4,4608]{2,1,0:T(4,128)(2,1)S(1)} async-done(((bf16[16,4,4608]{2,1,0:T(4,128)(2,1)}), bf16[16,4,4608]{2,1,0:T(4,128)(2,1)S(1)}, u32[]{:S(2)}, u32[]{:S(2)}) %all-to-all-start.1) | async-done | bytes 589856 | tf_op jit(solution)/shard_map/all_to_all | solution.py:202
  75.0 1.8 %increments.1 = f32[4,8,9216]{2,1,0:T(8,128)} custom-call(bf16[16,4,4608]{2,1,0:T(4,128)(2,1)S(1)} %all-to-all-done.1.ladder_ref, f32[4,8,9216]{2,1,0:T(8,128)S(1)} %get-tuple-element.21.scale_ref, f32[4,8,9216]{2,1,0:T(8,128)S(1)} %get-tuple-element.22.offset_ref), custom_call_target="tpu_custom_call" | custom-call | tf_op jit(solution)/shard_map/increments/pallas_call | solution.py:167
  (11 shorter events, 0.0 us)
Async XLA Ops:
  0.0 11.7 %copy-start = (f32[8,96,96]{2,1,0:T(8,128)S(1)}, f32[8,96,96]{2,1,0:T(8,128)}, u32[]{:S(2)}) copy-start(f32[8,96,96]{2,1,0:T(8,128)} %param.9) | copy-start | bytes 884740
  0.0 8.2 %copy-start.1 = (s32[8]{0:T(128)S(1)}, s32[8]{0:T(128)}, u32[]{:S(2)}) copy-start(s32[8]{0:T(128)} %sizes_ref.3) | copy-start | bytes 100
  2.3 6.4 %copy-start.2 = (f32[4,8,9216]{2,1,0:T(8,128)S(1)}, f32[4,8,9216]{2,1,0:T(8,128)}, u32[]{:S(2)}) copy-start(f32[4,8,9216]{2,1,0:T(8,128)} %amps_ref.1) | copy-start | bytes 3538948
  2.3 18.4 %all-to-all-start = ((bf16[8,4,9216]{2,1,0:T(4,128)(2,1)}), bf16[8,4,9216]{2,1,0:T(4,128)(2,1)S(1)}, u32[]{:S(2)}, u32[]{:S(2)}) async-start(bf16[8,4,9216]{2,1,0:T(4,128)(2,1)} %block_copies.1), calls=%async_computation | async-start | bytes 1179648 | tf_op jit(solution)/shard_map/all_to_all | solution.py:185
  20.2 34.0 %copy-start.4 = (f32[150]{0:T(256)S(1)}, f32[150]{0:T(256)}, u32[]{:S(2)}) copy-start(f32[150]{0:T(256)} %param.11) | copy-start | bytes 1804
  20.2 34.0 %copy-start.5 = (s32[4,2]{0,1:T(2,128)S(1)}, s32[4,2]{0,1:T(2,128)}, u32[]{:S(2)}) copy-start(s32[4,2]{0,1:T(2,128)} %param.13) | copy-start | bytes 100
  20.7 4.9 %collective-permute-start = (bf16[8,4,9216]{2,1,0:T(4,128)(2,1)S(1)}, bf16[8,4,9216]{2,1,0:T(4,128)(2,1)S(1)}, u32[]{:S(2)}, u32[]{:S(2)}) collective-permute-start(bf16[8,4,9216]{2,1,0:T(4,128)(2,1)S(1)} %all-to-all-done.own_ref), channel_id=1, source_target_pairs={{0,1},{1,0},{2,3},{3,2},{4,5},{5,4},{6,7},{7,6},{8,9},{9,8},{10,11... | collective-permute-start | bytes 1769480 | tf_op jit(solution)/shard_map/ppermute | solution.py:196
  54.2 5.2 %copy-start.3 = (f32[8,96]{1,0:T(8,128)S(1)}, f32[8,96]{1,0:T(8,128)}, u32[]{:S(2)}) copy-start(f32[8,96]{1,0:T(8,128)} %param.10) | copy-start | bytes 9220
  54.4 20.5 %all-to-all-start.1 = ((bf16[16,4,4608]{2,1,0:T(4,128)(2,1)}), bf16[16,4,4608]{2,1,0:T(4,128)(2,1)S(1)}, u32[]{:S(2)}, u32[]{:S(2)}) async-start(bf16[16,4,4608]{2,1,0:T(4,128)(2,1)} %ladder_rows.1), calls=%async_computation.1 | async-start | bytes 1179648 | tf_op jit(solution)/shard_map/all_to_all | solution.py:202
where the time goes:
time: 77.6 us; the launch traced here: 76.8 us
  Pallas kernels  32.7 us (42%)
  waiting for transfers between devices  14.9 us (19%)
  starting transfers between devices  14.2 us (18%)
  local copies, waits for them, and re-layouts  7.41 us (10%)
  matrix products  4.17 us (5%)
  other arithmetic  3.23 us (4%)
    pallas_call x1, Pallas kernels, ladder_rows(): pl.pallas_call(functools.partial(ladder_kernel, orbitals=orbitals, stripe...  28.6 us
    all_to_all x1, waiting for transfers between devices, on_device(): ladder = lax.all_to_all(sent, 'pair', split_axis=0, concat_axis=0)  12.9 us
    all_to_all x1, starting transfers between devices, on_device(): lax.all_to_all(copies, 'pair', split_axis=0, concat_axis=0, axis_index_gr...  5.86 us
    all_to_all x1, starting transfers between devices, on_device(): ladder = lax.all_to_all(sent, 'pair', split_axis=0, concat_axis=0)  5.01 us
    reshape x2, local copies, waits for them, and re-layouts, on_device(): fock = fock.reshape(pair_count, irreps, square)  4.27 us
    ppermute x1, starting transfers between devices, on_device(): other = lax.ppermute(own, 'pair', other_core)  3.28 us
    dot_general x1, matrix products, on_device(): jnp.einsum('hac,phcb->phab', fock_vv, amps, precision=lax.Precision.HIGHEST)  2.67 us
    pallas_call x1, Pallas kernels, block_copies(): pl.pallas_call(functools.partial(block_kernel, width=width), in_specs=[AN...  2.28 us
  transfers between devices with their start and end apart: 3, of which 3 were waited for; matrix products, arithmetic and copies ran while one was open for 19% of the time, Pallas kernels for 0%

commit v1 on v0

--- a/solution.py
+++ b/solution.py
@@ -56,7 +56,29 @@
     )(sizes, amps)
 
 
-def ladder_kernel(sizes_ref, own_ref, other_ref, ints_ref, out_ref, amps, slots, total, arrived, *, orbitals, stripe):
+def head_kernel(ints_ref, head_ref, arrived):
+    copy = pltpu.make_async_copy(ints_ref.at[pl.ds(0, head_ref.shape[0])], head_ref, arrived)
+    copy.start()
+    copy.wait()
+
+
+def head_of(ints, rows):
+    columns = ints.shape[1]
+    return pl.pallas_call(
+        head_kernel,
+        in_specs=[ANYWHERE],
+        out_specs=IN_VMEM,
+        out_shape=pltpu.VMEM((rows, columns), ints.dtype),
+        scratch_shapes=[pltpu.SemaphoreType.DMA],
+        compiler_params=pltpu.CompilerParams(vmem_limit_bytes=4 * 1024 * 1024),
+        cost_estimate=pl.CostEstimate(
+            flops=0, bytes_accessed=4 * rows * columns, transcendentals=0
+        ),
+        name="head_of_integrals",
+    )(ints)
+
+
+def ladder_kernel(sizes_ref, own_ref, other_ref, head_ref, ints_ref, out_ref, amps, slots, total, arrived, *, orbitals, stripe):
     depth, tile, columns = slots.shape
     tiles = out_ref.shape[2] // tile
     each = out_ref.shape[1]
@@ -75,8 +97,8 @@
         )
 
     def begin(width):
-        for slot in range(min(depth - 1, tiles)):
-            fetch(width, slot, slot).start()
+        for place in range(1, min(depth, tiles)):
+            fetch(width, place % depth, place).start()
 
     def store(place):
         ladder = total[...].T
@@ -95,7 +117,7 @@
             def _():
                 fetch(width, lax.rem(place + depth - 1, depth), place + depth - 1).start()
 
-            store(jnp.maximum(place - 1, 0))
+            store(place - 1)
             total[...] = lax.dot_general(
                 slots[slot, :, :width],
                 amps[:, :width],
@@ -104,7 +126,13 @@
             )
             return carry
 
-        lax.fori_loop(0, tiles, item, 0)
+        total[...] = lax.dot_general(
+            head_ref[:, :width],
+            amps[:, :width],
+            CONTRACT_LAST,
+            preferred_element_type=jnp.float32,
+        )
+        lax.fori_loop(1, tiles, item, 0)
 
     for count in range(least, most + 1):
         pl.when(steps == count)(functools.partial(begin, count * stripe))
@@ -113,21 +141,21 @@
     other = other_ref[...].astype(jnp.float32)
     both = [jnp.where(core == 0, own, other), jnp.where(core == 0, other, own)]
     amps[...] = jnp.concatenate(both, axis=1).reshape(amps.shape).astype(amps.dtype)
-    total[...] = jnp.zeros_like(total)
     for count in range(least, most + 1):
         pl.when(steps == count)(functools.partial(run, count * stripe))
     store(tiles - 1)
 
 
-def ladder_rows(sizes, own, other, ints, orbitals):
+def ladder_rows(sizes, own, other, head, ints, orbitals):
     chips, each, columns = own.shape
     pairs = 2 * chips * each
     rows = ints.shape[0]
-    tile = tile_of(rows, 256)
+    tile = head.shape[0]
     depth = 4 if tile <= 256 else 3
+    need = 2 * depth * tile * columns + 12 * pairs * columns + 4 * 1024 * 1024
     return pl.pallas_call(
         functools.partial(ladder_kernel, orbitals=orbitals, stripe=columns // 12),
-        in_specs=[IN_SMEM, IN_VMEM, IN_VMEM, ANYWHERE],
+        in_specs=[IN_SMEM, IN_VMEM, IN_VMEM, IN_VMEM, ANYWHERE],
         out_specs=IN_VMEM,
         out_shape=jax.ShapeDtypeStruct((2 * chips, each, rows), jnp.bfloat16),
         scratch_shapes=[
@@ -136,12 +164,12 @@
             pltpu.VMEM((tile, pairs), jnp.float32),
             pltpu.SemaphoreType.DMA((depth,)),
         ],
-        compiler_params=pltpu.CompilerParams(vmem_limit_bytes=VMEM_BYTES),
+        compiler_params=pltpu.CompilerParams(vmem_limit_bytes=min(VMEM_BYTES, need)),
         cost_estimate=pl.CostEstimate(
             flops=2 * pairs * rows * columns, bytes_accessed=2 * rows * columns, transcendentals=0
         ),
         name="ladder_rows",
-    )(sizes, own, other, ints)
+    )(sizes, own, other, head, ints)
 
 
 def increment_kernel(ladder_ref, scale_ref, offset_ref, out_ref):
@@ -192,9 +220,10 @@
     fock = jnp.einsum("phac,hcb->phab", amps, fock_vv, precision=lax.Precision.HIGHEST)
     fock = fock + jnp.einsum("hac,phcb->phab", fock_vv, amps, precision=lax.Precision.HIGHEST)
     fock = fock.reshape(pair_count, irreps, square)
-    own, fock = lax.optimization_barrier((own, fock))
+    own, fock, ladder_ints = lax.optimization_barrier((own, fock, ladder_ints))
     other = lax.ppermute(own, "pair", other_core)
-    sent = ladder_rows(vir_sizes, own, other, ladder_ints, width)
+    head = head_of(ladder_ints, tile_of(ladder_ints.shape[0], 256))
+    sent = ladder_rows(vir_sizes, own, other, head, ladder_ints, width)
 
     sent, fock, vir_energy, occ_energy = lax.optimization_barrier(
         (sent, fock, vir_energy, occ_energy)

time: 77.6 us -> 73 us (0.941)
  Pallas kernels: 32.7 us -> 30 us
  waiting for transfers between devices: 14.9 us -> 13.3 us
    pallas_call x1, Pallas kernels: 28.6 us -> 23.5 us  [ladder_rows(): pl.pallas_call(functools.partial(ladder_kernel, orbitals=orbitals, stripe...]
    pallas_call x0 -> x1, Pallas kernels: none -> 2.34 us  [head_of(): pl.pallas_call(head_kernel, in_specs=[ANYWHERE], out_specs=IN_VMEM, out_s...]
    ppermute x1, waiting for transfers between devices: 1.63 us -> 0.01 us  [on_device(): other = lax.ppermute(own, 'pair', other_core)]
  transfers between devices with their start and end apart: 3 -> 3, of which waited for: 3 -> 2; matrix products, arithmetic and copies ran while one was open for 19% -> 20% of each run, Pallas kernels for 0% -> 3%
where the time goes in v1:
time: 73 us; the launch traced here: 72.2 us
  Pallas kernels  30 us (41%)
  starting transfers between devices  13.9 us (19%)
  waiting for transfers between devices  13.3 us (18%)
  local copies, waits for them, and re-layouts  7.42 us (10%)
  matrix products  4.18 us (6%)
  other arithmetic  3.23 us (4%)
    pallas_call x1, Pallas kernels, ladder_rows(): pl.pallas_call(functools.partial(ladder_kernel, orbitals=orbitals, stripe...  23.5 us
    all_to_all x1, waiting for transfers between devices, on_device(): ladder = lax.all_to_all(sent, 'pair', split_axis=0, concat_axis=0)  12.9 us
    all_to_all x1, starting transfers between devices, on_device(): lax.all_to_all(copies, 'pair', split_axis=0, concat_axis=0, axis_index_gr...  5.86 us
    all_to_all x1, starting transfers between devices, on_device(): ladder = lax.all_to_all(sent, 'pair', split_axis=0, concat_axis=0)  4.75 us
    reshape x2, local copies, waits for them, and re-layouts, on_device(): fock = fock.reshape(pair_count, irreps, square)  4.27 us
    ppermute x1, starting transfers between devices, on_device(): other = lax.ppermute(own, 'pair', other_core)  3.28 us
    dot_general x1, matrix products, on_device(): jnp.einsum('hac,phcb->phab', fock_vv, amps, precision=lax.Precision.HIGHEST)  2.67 us
    pallas_call x1, Pallas kernels, head_of(): pl.pallas_call(head_kernel, in_specs=[ANYWHERE], out_specs=IN_VMEM, out_s...  2.34 us
  transfers between devices with their start and end apart: 3, of which 2 were waited for; matrix products, arithmetic and copies ran while one was open for 20% of the time, Pallas kernels for 3%

profile of v1, /device:TPU:11, one launch (start us, length us, event | category | flops | bytes accessed | tf_op | source)
XLA Modules:
  0.0 72.2 jit_solution(7198885003371413166)
XLA Ops:
  0.0 2.3 %block_copies.1 = bf16[8,4,9216]{2,1,0:T(4,128)(2,1)} custom-call(s32[8]{0:T(128)} %sizes_ref.3, f32[4,8,9216]{2,1,0:T(8,128)} %amps_ref.1), custom_call_target="tpu_custom_call" | custom-call | tf_op jit(solution)/shard_map/block_copies/pallas_call | solution.py:44
  2.3 0.0 copy-start.2
  2.3 5.9 %all-to-all-start = ((bf16[8,4,9216]{2,1,0:T(4,128)(2,1)}), bf16[8,4,9216]{2,1,0:T(4,128)(2,1)S(1)}, u32[]{:S(2)}, u32[]{:S(2)}) async-start(bf16[8,4,9216]{2,1,0:T(4,128)(2,1)} %block_copies.1), calls=%async_computation | async-start | bytes 1179648 | tf_op jit(solution)/shard_map/all_to_all | solution.py:213
  8.2 0.1 iota_compare_fusion.1
  8.2 0.2 broadcast_and_fusion
  8.4 0.3 and.23
  8.7 1.1 %broadcast_select_fusion = f32[4,8,9216]{2,1,0:T(8,128)} fusion(f32[4,8,9216]{2,1,0:T(8,128)S(1)} %copy-done.2, pred[8,9216]{1,0:T(8,128)(4,1)S(1)} %and.23), kind=kLoop, calls=%fused_computation.5 | loop fusion | flops 294912 | bytes 2433024 | tf_op jit(solution)/shard_map/jit(_where)/select_n | solution.py:218
  9.8 1.9 %reshape.84 = f32[4,8,96,96]{3,2,1,0:T(8,128)S(1)} reshape(f32[4,8,9216]{2,1,0:T(8,128)} %broadcast_select_fusion) | data formatting | bytes 2359296 | tf_op jit(solution)/shard_map/reshape | solution.py:219
  11.7 1.5 %fusion.1 = f32[8,4,96,96]{3,2,1,0:T(8,128)S(1)} fusion(f32[4,8,96,96]{3,2,1,0:T(8,128)S(1)} %reshape.84, f32[8,96,96]{2,1,0:T(8,128)S(1)} %copy-done), kind=kOutput, calls=%fused_computation.2 | convolution fusion | flops 339738624 | bytes 2654208 | tf_op jit(solution)/shard_map/phac,hcb->phab/dot_general | solution.py:220
  13.3 2.7 %bitcast_add_fusion = f32[4,8,96,96]{3,2,0,1:T(8,128)} fusion(f32[8,4,96,96]{3,2,1,0:T(8,128)S(1)} %fusion.1, f32[4,8,96,96]{3,2,1,0:T(8,128)S(1)} %reshape.84, f32[8,96,96]{2,1,0:T(8,128)S(1)} %copy-done), kind=kOutput, calls=%fused_computation | convolution fusion | flops 340033536 | bytes 3833856 | tf_op jit(solution)/shard_map/hac,phcb->phab/dot_general | solution.py:221
  15.9 2.6 %reshape.87 = f32[4,8,9216]{2,0,1:T(4,128)S(1)} reshape(f32[4,8,96,96]{3,2,0,1:T(8,128)} %bitcast_add_fusion) | data formatting | bytes 2359296 | tf_op jit(solution)/shard_map/reshape | solution.py:222
  18.5 1.7 %copy.21 = f32[4,8,9216]{2,1,0:T(8,128)} copy(f32[4,8,9216]{2,0,1:T(4,128)S(1)} %reshape.87) | data formatting | bytes 2359296 | tf_op jit(solution)/shard_map/reshape | solution.py:222
  20.2 0.5 all-to-all-done.own_ref
  20.7 3.3 %collective-permute-start = (bf16[8,4,9216]{2,1,0:T(4,128)(2,1)S(1)}, bf16[8,4,9216]{2,1,0:T(4,128)(2,1)S(1)}, u32[]{:S(2)}, u32[]{:S(2)}) collective-permute-start(bf16[8,4,9216]{2,1,0:T(4,128)(2,1)S(1)} %all-to-all-done.own_ref), channel_id=1, source_target_pairs={{0,1},{1,0},{2,3},{3,2},{4,5},{5,4},{6,7},{7,6},{8,9},{9,8},{10,11... | collective-permute-start | bytes 1769480 | tf_op jit(solution)/shard_map/ppermute | solution.py:224
  23.9 2.3 %head_of_integrals.1.head_ref = bf16[256,9216]{1,0:T(8,128)(2,1)S(1)} custom-call(bf16[4608,9216]{1,0:T(8,128)(2,1)} %ints_ref.1), custom_call_target="tpu_custom_call" | custom-call | bytes 9437184 | tf_op jit(solution)/shard_map/head_of_integrals/pallas_call | solution.py:67
  26.3 0.0 copy-start.4
  26.3 23.5 %ladder_rows.1 = bf16[16,4,4608]{2,1,0:T(4,128)(2,1)} custom-call(s32[8]{0:T(128)S(1)} %copy-done.1, bf16[8,4,9216]{2,1,0:T(4,128)(2,1)S(1)} %all-to-all-done.own_ref, bf16[8,4,9216]{2,1,0:T(4,128)(2,1)S(1)} %collective-permute-done.other_ref, bf16[256,9216]{1,0:T(8,128)(2,1)S(1)} %head_of_integrals.1.head_ref, bf16[4608,9216]{1,0:T(8,128)(2,1)} %ints_ref.1), custom_call_target="tpu_custom_call" | custom-call | flops 5435817984 | bytes 84934656 | tf_op jit(solution)/shard_map/ladder_rows/pallas_call | solution.py:156
  49.9 0.2 select_reduce_fusion
  50.1 4.8 %all-to-all-start.1 = ((bf16[16,4,4608]{2,1,0:T(4,128)(2,1)}), bf16[16,4,4608]{2,1,0:T(4,128)(2,1)S(1)}, u32[]{:S(2)}, u32[]{:S(2)}) async-start(bf16[16,4,4608]{2,1,0:T(4,128)(2,1)} %ladder_rows.1), calls=%async_computation.1 | async-start | bytes 1179648 | tf_op jit(solution)/shard_map/all_to_all | solution.py:231
  54.8 0.2 broadcast_add_fusion
  55.0 0.9 %add.37 = f32[8,9216]{1,0:T(8,128)} reshape(f32[8,96,96]{2,1,0:T(8,128)S(1)} %broadcast_add_fusion) | data formatting | bytes 589824 | tf_op jit(solution)/shard_map/add | solution.py:238
  55.9 1.6 %fusion.5 = (f32[4,8,9216]{2,1,0:T(8,128)S(1)}, f32[4,8,9216]{2,1,0:T(8,128)S(1)}) fusion(f32[4,8,9216]{2,1,0:T(8,128)} %copy.21, f32[4]{0:T(128)S(1)} %add_bitcast_fusion, f32[8,9216]{1,0:T(8,128)} %add.37, pred[8,9216]{1,0:T(8,128)(4,1)S(1)} %and.23), kind=kLoop, calls=%fused_computation.10 | loop fusion | flops 1179648 | bytes 3907600 | tf_op jit(solution)/shard_map/mul | solution.py:241
  57.5 12.9 %all-to-all-done.1.ladder_ref = bf16[16,4,4608]{2,1,0:T(4,128)(2,1)S(1)} async-done(((bf16[16,4,4608]{2,1,0:T(4,128)(2,1)}), bf16[16,4,4608]{2,1,0:T(4,128)(2,1)S(1)}, u32[]{:S(2)}, u32[]{:S(2)}) %all-to-all-start.1) | async-done | bytes 589856 | tf_op jit(solution)/shard_map/all_to_all | solution.py:231
  70.4 1.8 %increments.1 = f32[4,8,9216]{2,1,0:T(8,128)} custom-call(bf16[16,4,4608]{2,1,0:T(4,128)(2,1)S(1)} %all-to-all-done.1.ladder_ref, f32[4,8,9216]{2,1,0:T(8,128)S(1)} %get-tuple-element.23.scale_ref, f32[4,8,9216]{2,1,0:T(8,128)S(1)} %get-tuple-element.24.offset_ref), custom_call_target="tpu_custom_call" | custom-call | tf_op jit(solution)/shard_map/increments/pallas_call | solution.py:195
  (12 shorter events, 0.0 us)
Async XLA Ops:
  0.0 11.7 %copy-start = (f32[8,96,96]{2,1,0:T(8,128)S(1)}, f32[8,96,96]{2,1,0:T(8,128)}, u32[]{:S(2)}) copy-start(f32[8,96,96]{2,1,0:T(8,128)} %param.9) | copy-start | bytes 884740
  0.0 8.2 %copy-start.1 = (s32[8]{0:T(128)S(1)}, s32[8]{0:T(128)}, u32[]{:S(2)}) copy-start(s32[8]{0:T(128)} %sizes_ref.3) | copy-start | bytes 100
  2.3 6.4 %copy-start.2 = (f32[4,8,9216]{2,1,0:T(8,128)S(1)}, f32[4,8,9216]{2,1,0:T(8,128)}, u32[]{:S(2)}) copy-start(f32[4,8,9216]{2,1,0:T(8,128)} %amps_ref.1) | copy-start | bytes 3538948
  2.3 18.4 %all-to-all-start = ((bf16[8,4,9216]{2,1,0:T(4,128)(2,1)}), bf16[8,4,9216]{2,1,0:T(4,128)(2,1)S(1)}, u32[]{:S(2)}, u32[]{:S(2)}) async-start(bf16[8,4,9216]{2,1,0:T(4,128)(2,1)} %block_copies.1), calls=%async_computation | async-start | bytes 1179648 | tf_op jit(solution)/shard_map/all_to_all | solution.py:213
  20.7 5.7 %collective-permute-start = (bf16[8,4,9216]{2,1,0:T(4,128)(2,1)S(1)}, bf16[8,4,9216]{2,1,0:T(4,128)(2,1)S(1)}, u32[]{:S(2)}, u32[]{:S(2)}) collective-permute-start(bf16[8,4,9216]{2,1,0:T(4,128)(2,1)S(1)} %all-to-all-done.own_ref), channel_id=1, source_target_pairs={{0,1},{1,0},{2,3},{3,2},{4,5},{5,4},{6,7},{7,6},{8,9},{9,8},{10,11... | collective-permute-start | bytes 1769480 | tf_op jit(solution)/shard_map/ppermute | solution.py:224
  26.3 23.6 %copy-start.4 = (f32[150]{0:T(256)S(1)}, f32[150]{0:T(256)}, u32[]{:S(2)}) copy-start(f32[150]{0:T(256)} %param.11) | copy-start | bytes 1804
  26.3 23.6 %copy-start.5 = (s32[4,2]{0,1:T(2,128)S(1)}, s32[4,2]{0,1:T(2,128)}, u32[]{:S(2)}) copy-start(s32[4,2]{0,1:T(2,128)} %param.13) | copy-start | bytes 100
  49.9 4.9 %copy-start.3 = (f32[8,96]{1,0:T(8,128)S(1)}, f32[8,96]{1,0:T(8,128)}, u32[]{:S(2)}) copy-start(f32[8,96]{1,0:T(8,128)} %param.10) | copy-start | bytes 9220
  50.1 20.3 %all-to-all-start.1 = ((bf16[16,4,4608]{2,1,0:T(4,128)(2,1)}), bf16[16,4,4608]{2,1,0:T(4,128)(2,1)S(1)}, u32[]{:S(2)}, u32[]{:S(2)}) async-start(bf16[16,4,4608]{2,1,0:T(4,128)(2,1)} %ladder_rows.1), calls=%async_computation.1 | async-start | bytes 1179648 | tf_op jit(solution)/shard_map/all_to_all | solution.py:231
